TPU v7x, 512 devices: a whole 4x8x8 slice. The times are simulated.
512 devices in a mesh: seq: 64 (over y, z), mp: 8 (over x, core).
Axes of the slice: x: 4, y: 8, z: 8, core: 2. Of those that a mesh axis runs over, the one named last changes fastest.
Arguments:
- hidden: bfloat16 [8192, 4096], P('seq', 'mp'), may hold values from -24 to 24
- keys: bfloat16 [8192, 1024], P('seq', 'mp'), may hold values from -3000 to 3000
- values: bfloat16 [8192, 1024], P('seq', 'mp'), may hold values from -24 to 24
- norm_gain: float32 [4096], P('mp'), may hold values from 0.1 to 1.9
- w_query: bfloat16 [4096, 2048], P('mp'), may hold values from -0.09375 to 0.09375
- w_out: bfloat16 [2048, 4096], P(None, 'mp'), may hold values from -0.25 to 0.25
- depth: int32 [64], P('seq'), may hold values from 1 to 3
- cotangent: bfloat16 [8192, 4096], P('seq', 'mp'), may hold values from -6 to 6
Outputs:
- mixed: bfloat16 [8192, 4096], P('seq', 'mp')
- grad_hidden: bfloat16 [8192, 4096], P('seq', 'mp')
All inputs are finite; a program needn't handle non-finite values.
Results may differ from a plain program's by a relative error of at most 0.04.
Values may be sent and summed in bfloat16 or wider, within the bound.
A program may use at most 64 MiB of HBM per device.

v0:
```python
import jax
import jax.numpy as jnp
from jax import lax
from jax.sharding import PartitionSpec as P

D = 4096
HQ = 16
KVH = 8
HD = 128
BLOCK = 128


epsilon = 1e-05
very_low = -1e30


def arrange_heads(rows, kv_local):
    n_rows = rows.shape[0]
    shaped = rows.reshape(n_rows, kv_local, HQ // KVH, HD)
    return jnp.transpose(shaped, (1, 2, 0, 3)).reshape(kv_local, HQ // KVH * n_rows, HD)


def restore_heads(grouped, n_rows):
    kv_local = grouped.shape[0]
    shaped = grouped.reshape(kv_local, HQ // KVH, n_rows, HD)
    return jnp.transpose(shaped, (2, 0, 1, 3)).reshape(n_rows, kv_local * (HQ // KVH) * HD)


def piece_scores(queries, key_piece, key_start, query_pos):
    count = key_piece.shape[0]
    kv_local = queries.shape[0]
    keys_h = key_piece.reshape(count, kv_local, HD)
    scores = jnp.einsum(
        "kqd,nkd->kqn", queries, keys_h, preferred_element_type=jnp.float32
    ) * HD ** (-0.5)
    key_pos = key_start + jnp.arange(count, dtype=jnp.int32)
    allowed = key_pos[None, :] <= query_pos[:, None]
    return (scores, allowed, keys_h)


def forward_piece(carry, queries, query_pos, key_piece, value_piece, key_start):
    best, total, accum = carry
    scores, allowed, keys_h = piece_scores(queries, key_piece, key_start, query_pos)
    values_h = value_piece.reshape(key_piece.shape[0], queries.shape[0], HD)
    block_best = jnp.max(jnp.where(allowed, scores, very_low), axis=2)
    weights = jnp.where(allowed, jnp.exp(scores - block_best[:, :, None]), 0.0)
    block_total = jnp.sum(weights, axis=2)
    block_accum = jnp.einsum(
        "kqn,nkd->kqd", weights.astype(jnp.bfloat16), values_h, preferred_element_type=jnp.float32
    )
    merged = jnp.maximum(best, block_best)
    new_scale = jnp.exp(block_best - merged)
    return (merged, block_total * new_scale, block_accum * new_scale[:, :, None])


def backward_piece(
    accum,
    queries,
    grad_grouped,
    deltas,
    logsum,
    live_grouped,
    query_pos,
    key_piece,
    value_piece,
    key_start,
):
    scores, allowed, keys_h = piece_scores(queries, key_piece, key_start, query_pos)
    values_h = value_piece.reshape(key_piece.shape[0], queries.shape[0], HD)
    allowed = allowed & live_grouped[:, None]
    probs = jnp.where(allowed, jnp.exp(scores - logsum[:, :, None]), 0.0)
    dprobs = jnp.einsum("kqd,nkd->kqn", grad_grouped, values_h, preferred_element_type=jnp.float32)
    dscores = (probs * (dprobs - deltas[:, :, None])).astype(jnp.bfloat16)
    return accum + jnp.einsum("kqn,nkd->kqd", dscores, keys_h, preferred_element_type=jnp.float32)


def run_blocks(piece_fn, carry, whole_keys, whole_values, used, block):

    def turn(index, state):
        start = index * block
        key_part = lax.dynamic_slice_in_dim(whole_keys, start, block, 0)
        value_part = lax.dynamic_slice_in_dim(whole_values, start, block, 0)
        return piece_fn(state, key_part, value_part, start)

    return lax.fori_loop(0, used, turn, carry)


def shards(hidden, keys, values, norm_gain, w_query, w_out, depth, cotangent):
    tok = hidden.shape[0]
    kv_local = keys.shape[1] // HD
    groups = HQ // KVH
    first_row = lax.axis_index("seq") * tok
    last_row = first_row + tok - 1
    own_pos = first_row + jnp.arange(tok, dtype=jnp.int32)
    query_pos = jnp.tile(own_pos, groups)
    block_depth = jnp.repeat(depth, BLOCK)
    whole_len = tok * lax.axis_size("seq")
    block = min(512, whole_len)
    grouped_rows = groups * tok
    whole = None
    state = hidden
    saved = []
    for level in (2, 3):
        live_rows = block_depth >= level
        live_float = live_rows.astype(jnp.float32)
        live_any = jnp.any(live_rows)
        live_grouped = jnp.tile(live_rows, groups)
        used = jnp.where(live_any, last_row // block + 1, 0)
        state_f = state.astype(jnp.float32)
        squares = lax.psum(jnp.sum(state_f * state_f, axis=1), "mp")
        inverse = lax.rsqrt(squares / D + epsilon)
        normed = (state_f * inverse[:, None] * norm_gain[None, :]).astype(jnp.bfloat16)
        partial_value = jnp.dot(normed, w_query, preferred_element_type=jnp.float32)
        query = lax.psum_scatter(
            partial_value.astype(jnp.bfloat16), "mp", scatter_dimension=1, tiled=True
        )
        grouped = arrange_heads(query, kv_local)
        init = (
            jnp.full((kv_local, grouped_rows), very_low, jnp.float32),
            jnp.zeros((kv_local, grouped_rows), jnp.float32),
            jnp.zeros((kv_local, grouped_rows, HD), jnp.float32),
        )

        def forward_fn(carry, key_piece, value_piece, start, grouped=grouped):
            return forward_piece(carry, grouped, query_pos, key_piece, value_piece, start)

        def fold_fn(carry, pieces, start, forward_fn=forward_fn, live_any=live_any):
            return lax.cond(
                live_any & (start <= last_row),
                lambda inner: forward_fn(inner, pieces[0], pieces[1], start),
                lambda inner: inner,
                carry,
            )

        best, total, accum = fold_fn(
            init,
            (
                lax.all_gather(keys, "seq", axis=0, tiled=True),
                lax.all_gather(values, "seq", axis=0, tiled=True),
            ),
            jnp.int32(0),
        )
        safe_total = jnp.where(live_grouped[None, :], total, 1.0)
        attended = (accum / safe_total[:, :, None]).astype(jnp.bfloat16)
        logsum = best + jnp.log(safe_total)
        flat = restore_heads(attended, tok)
        mixed_rows = jnp.dot(
            lax.all_gather(flat, "mp", axis=1, tiled=True),
            w_out,
            preferred_element_type=jnp.float32,
        )
        saved.append((state, inverse, grouped, attended, logsum, live_float, live_grouped, used))
        state = (state_f + live_float[:, None] * mixed_rows).astype(jnp.bfloat16)
    whole = (
        lax.all_gather(keys, "seq", axis=0, tiled=True),
        lax.all_gather(values, "seq", axis=0, tiled=True),
    )
    grad = cotangent
    for entry in reversed(saved):
        state_in, inverse, grouped, attended, logsum, live_float, live_grouped, used = entry
        grad_f = grad.astype(jnp.float32)
        grad_mix = (grad_f * live_float[:, None]).astype(jnp.bfloat16)
        partial_value = lax.dot_general(
            grad_mix, w_out, (((1,), (1,)), ((), ())), preferred_element_type=jnp.float32
        )
        grad_heads = lax.psum_scatter(
            partial_value.astype(jnp.bfloat16), "mp", scatter_dimension=1, tiled=True
        )
        grad_grouped = arrange_heads(grad_heads, kv_local)
        deltas = jnp.sum(grad_grouped.astype(jnp.float32) * attended.astype(jnp.float32), axis=2)

        def back_fn(
            accum,
            key_piece,
            value_piece,
            start,
            grouped=grouped,
            grad_grouped=grad_grouped,
            deltas=deltas,
            logsum=logsum,
            live_grouped=live_grouped,
        ):
            return backward_piece(
                accum,
                grouped,
                grad_grouped,
                deltas,
                logsum,
                live_grouped,
                query_pos,
                key_piece,
                value_piece,
                start,
            )

        query_grad = run_blocks(
            back_fn,
            jnp.zeros((kv_local, grouped_rows, HD), jnp.float32),
            whole[0],
            whole[1],
            used,
            block,
        )
        query_rows = restore_heads((query_grad * HD ** (-0.5)).astype(jnp.bfloat16), tok)
        grad_normed = lax.dot_general(
            lax.all_gather(query_rows, "mp", axis=1, tiled=True),
            w_query,
            (((1,), (1,)), ((), ())),
            preferred_element_type=jnp.float32,
        )
        scaled = grad_normed * norm_gain[None, :]
        state_f = state_in.astype(jnp.float32)
        inner = lax.psum(jnp.sum(scaled * state_f, axis=1), "mp")
        grad_x = inverse[:, None] * scaled - state_f * (inverse**3 * inner / D)[:, None]
        grad = (grad_f + grad_x).astype(jnp.bfloat16)
    return (state, grad)


def solution(mesh):
    return jax.shard_map(
        shards,
        mesh=mesh,
        in_specs=(
            P("seq", "mp"),
            P("seq", "mp"),
            P("seq", "mp"),
            P("mp"),
            P("mp", None),
            P(None, "mp"),
            P("seq"),
            P("seq", "mp"),
        ),
        out_specs=(P("seq", "mp"), P("seq", "mp")),
        check_vma=False,
    )
```

profile of v0, /device:TPU:312, one launch (start us, length us, event | category | flops | bytes accessed | tf_op | source)
XLA Modules:
  0.0 483.6 jit_solution(12437761909602948301)
XLA Ops:
  9.2 14.6 %psum.28 = f32[128]{0:T(128)S(1)} all-reduce(f32[128]{0:T(128)S(1)} %fusion.101), channel_id=1, replica_groups=mesh['seq'=64,'mp'=8] {'mp'}, use_global_device_ids=true, to_apply=%region_1.2 | all-reduce | flops 128 | bytes 1024 | tf_op jit(solution)/shard_map/psum | solution.py:110
  23.9 2.2 convolution_convert_fusion.3
  28.0 3.2 convolution_convert_fusion.1
  31.3 30.5 %reduce-scatter.5.cloned.1.call-done = bf16[128,256]{1,0:T(8,128)(2,1)} async-done(((bf16[128,2048]{1,0:T(8,128)(2,1)}), bf16[128,256]{1,0:T(8,128)(2,1)}) %reduce-scatter.5.cloned.1.call-update) | async-done | bytes 65552 | tf_op jit(solution)/shard_map/reduce_scatter | solution.py:114
  63.2 45.7 %all-gather.3.cloned.1.call-done = bf16[8192,128]{1,0:T(8,128)(2,1)} async-done(((bf16[128,128]{1,0:T(8,128)(2,1)}), bf16[8192,128]{1,0:T(8,128)(2,1)}) %all-gather.3.cloned.1.call-update) | async-done | bytes 2097168 | tf_op jit(solution)/shard_map/all_gather | solution.py:138
  109.0 84.0 %all-gather.5.cloned.1.call-done = bf16[8192,128]{1,0:T(8,128)(2,1)} async-done(((bf16[128,128]{1,0:T(8,128)(2,1)}), bf16[8192,128]{1,0:T(8,128)(2,1)}) %all-gather.5.cloned.1.call-update) | async-done | bytes 2097168 | tf_op jit(solution)/shard_map/all_gather | solution.py:139
  193.0 8.2 %conditional.2 = (f32[1,256]{1,0:T(1,128)S(1)}, f32[1,256]{1,0:T(1,128)S(1)}, f32[1,256,128]{2,1,0:T(8,128)S(1)}) conditional(s32[]{:T(128)} %convert_element_type.122, () %tuple.32, (s32[2,128]{1,0:T(2,128)S(1)}, bf16[1,256,128]{2,1,0:T(8,128)(2,1)}, bf16[8192,128]{1,0:T(8,128)(2,1)}, bf16[8192,128]{1,0:T(8,128)(2,1)}) %tuple.33), branch_computations={%region_3.4_spmd, %region_4.7_spmd} | conditional | flops 1098941184 | bytes 37959732 | solution.py:128
  193.0 3.5 select_reduce_fusion
  196.5 2.3 fusion.15
  198.9 2.3 fusion.9
  202.0 13.4 %all_gather.24 = bf16[128,2048]{0,1:T(8,128)(2,1)S(1)} all-gather(bf16[128,256]{0,1:T(8,128)(2,1)S(1)} %bitcast.164), channel_id=1, replica_groups=mesh['seq'=64,'mp'=8] {'mp'}, dimensions={1}, use_global_device_ids=true | all-gather | bytes 589824 | tf_op jit(solution)/shard_map/all_gather | solution.py:148
  215.4 2.2 multiply_reduce_fusion.1
  217.6 14.7 %psum.29 = f32[128]{0:T(128)S(1)} all-reduce(f32[128]{0:T(128)S(1)} %get-tuple-element.270), channel_id=1, replica_groups=mesh['seq'=64,'mp'=8] {'mp'}, use_global_device_ids=true, to_apply=%region_8.9 | all-reduce | flops 128 | bytes 1024 | tf_op jit(solution)/shard_map/psum | solution.py:110
  234.7 33.4 %reduce-scatter.7.cloned.1.call-done = bf16[128,256]{1,0:T(8,128)(2,1)} async-done(((bf16[128,2048]{1,0:T(8,128)(2,1)}), bf16[128,256]{1,0:T(8,128)(2,1)}) %reduce-scatter.7.cloned.1.call-update) | async-done | bytes 65552 | tf_op jit(solution)/shard_map/reduce_scatter | solution.py:114
  270.8 13.1 %all_gather.26 = bf16[128,2048]{0,1:T(8,128)(2,1)S(1)} all-gather(bf16[128,256]{0,1:T(8,128)(2,1)S(1)} %bitcast.166), channel_id=1, replica_groups=mesh['seq'=64,'mp'=8] {'mp'}, dimensions={1}, use_global_device_ids=true | all-gather | bytes 589824 | tf_op jit(solution)/shard_map/all_gather | solution.py:206
  284.8 12.8 %psum.30 = f32[128]{0:T(128)S(1)} all-reduce(f32[128]{0:T(128)S(1)} %get-tuple-element.272), channel_id=1, replica_groups=mesh['seq'=64,'mp'=8] {'mp'}, use_global_device_ids=true, to_apply=%region_19.20 | all-reduce | flops 128 | bytes 1024 | tf_op jit(solution)/shard_map/psum | solution.py:213
  297.7 3.2 convolution_convert_fusion
  301.1 13.1 %all_gather.25 = bf16[128,2048]{0,1:T(8,128)(2,1)S(1)} all-gather(bf16[128,256]{0,1:T(8,128)(2,1)S(1)} %bitcast.167), channel_id=1, replica_groups=mesh['seq'=64,'mp'=8] {'mp'}, dimensions={1}, use_global_device_ids=true | all-gather | bytes 589824 | tf_op jit(solution)/shard_map/all_gather | solution.py:148
  314.2 2.7 fusion.96
  317.0 86.6 %reduce-scatter.11.cloned.1.call-done = bf16[128,256]{1,0:T(8,128)(2,1)} async-done(((bf16[128,2048]{1,0:T(8,128)(2,1)}), bf16[128,256]{1,0:T(8,128)(2,1)}) %reduce-scatter.11.cloned.1.call-update) | async-done | bytes 65552 | tf_op jit(solution)/shard_map/reduce_scatter | solution.py:166
  404.7 44.0 %while.23 = (s32[]{:T(128)}, f32[1,256,128]{2,1,0:T(8,128)S(1)}, s32[]{:T(128)}, bf16[8192,128]{1,0:T(8,128)(2,1)}, bf16[1,256,128]{2,1,0:T(8,128)(2,1)}, /*inde...) while((s32[]{:T(128)}, f32[1,256,128]{2,1,0:T(8,128)S(1)}, ...), condition=%wide.region_23.24_spmd.clone, body=%wide.region_22.23_spmd.clone.sunk | while | flops 101745152 | bytes 1845443 | solution.py:85
  408.6 1.6 fusion.162
  411.4 1.6 fusion.162
  414.2 1.6 fusion.162
  416.9 1.6 fusion.162
  419.7 1.6 fusion.162
  425.2 1.6 fusion.162
  427.9 1.6 fusion.162
  436.2 1.6 fusion.162
  444.4 1.6 fusion.162
  448.9 13.1 %all_gather.27 = bf16[128,2048]{0,1:T(8,128)(2,1)S(1)} all-gather(bf16[128,256]{0,1:T(8,128)(2,1)S(1)} %bitcast.169), channel_id=1, replica_groups=mesh['seq'=64,'mp'=8] {'mp'}, dimensions={1}, use_global_device_ids=true | all-gather | bytes 589824 | tf_op jit(solution)/shard_map/all_gather | solution.py:206
  463.0 12.8 %psum.31 = f32[128]{0:T(128)S(1)} all-reduce(f32[128]{0:T(128)S(1)} %get-tuple-element.274), channel_id=1, replica_groups=mesh['seq'=64,'mp'=8] {'mp'}, use_global_device_ids=true, to_apply=%region_25.26 | all-reduce | flops 128 | bytes 1024 | tf_op jit(solution)/shard_map/psum | solution.py:213
  (140 shorter events, 43.0 us)
Async XLA Ops:
  8.0 15.9 %copy-start = (bf16[512,2048]{1,0:T(8,128)(2,1)S(1)}, bf16[512,2048]{1,0:T(8,128)(2,1)}, u32[]{:S(2)}) copy-start(bf16[512,2048]{1,0:T(8,128)(2,1)} %param.20) | copy-start | bytes 6291460
  8.0 20.0 %copy-start.4 = (bf16[128,512]{1,0:T(8,128)(2,1)S(1)}, bf16[128,512]{1,0:T(8,128)(2,1)}, u32[]{:S(2)}) copy-start(bf16[128,512]{1,0:T(8,128)(2,1)} %param.23) | copy-start | bytes 393220
  8.0 53.7 %reduce-scatter.5.cloned.1.call-start = ((), (), s32[]{:S(2)}) async-start(), calls=%async_computation.4 | async-start | bytes 589824 | tf_op jit(solution)/shard_map/reduce_scatter | solution.py:114
  23.8 7.3 %copy-start.11 = (f32[128]{0:T(128)}, f32[128]{0:T(128)S(1)}, u32[]{:S(2)}) copy-start(f32[128]{0:T(128)S(1)} %psum.28) | copy-start | bytes 1540
  23.9 7.3 %copy-start.6 = (f32[128]{0:T(128)}, f32[128]{0:T(128)S(1)}, u32[]{:S(2)}) copy-start(f32[128]{0:T(128)S(1)} %add_rsqrt_fusion.1) | copy-start | bytes 1540
  26.1 82.9 %all-gather.3.cloned.1.call-start = ((), (), s32[]{:S(2)}) async-start(), calls=%async_computation.5 | async-start | bytes 2129920 | tf_op jit(solution)/shard_map/all_gather | solution.py:138
  26.7 166.3 %all-gather.5.cloned.1.call-start = ((), (), s32[]{:S(2)}) async-start(), calls=%async_computation.6 | async-start | bytes 2129920 | tf_op jit(solution)/shard_map/all_gather | solution.py:139
  27.3 206.5 %reduce-scatter.9.cloned.1.call-start = ((), (), s32[]{:S(2)}) async-start(), calls=%async_computation.8 | async-start | bytes 589824 | tf_op jit(solution)/shard_map/reduce_scatter | solution.py:166
  31.2 236.9 %reduce-scatter.7.cloned.1.call-start = ((), (), s32[]{:S(2)}) async-start(), calls=%async_computation.7 | async-start | bytes 589824 | tf_op jit(solution)/shard_map/reduce_scatter | solution.py:114
  31.3 161.7 %copy-start.13 = (s32[128]{0:T(128)}, s32[128]{0:T(128)S(1)}, u32[]{:S(2)}) copy-start(s32[128]{0:T(128)S(1)} %iota_add_fusion.2) | copy-start | bytes 1540
  193.0 22.5 %copy-start.1 = (bf16[128,512]{1,0:T(8,128)(2,1)S(1)}, bf16[128,512]{1,0:T(8,128)(2,1)}, u32[]{:S(2)}) copy-start(bf16[128,512]{1,0:T(8,128)(2,1)} %param.16) | copy-start | bytes 393220
  193.0 3.5 copy-start.2
  201.2 31.2 %copy-start.5 = (f32[512]{0:T(512)S(1)}, f32[512]{0:T(512)}, u32[]{:S(2)}) copy-start(f32[512]{0:T(512)} %param.19) | copy-start | bytes 6148
  232.4 37.3 %copy-start.15 = (f32[128]{0:T(128)}, f32[128]{0:T(128)S(1)}, u32[]{:S(2)}) copy-start(f32[128]{0:T(128)S(1)} %psum.29) | copy-start | bytes 1540
  232.4 37.2 %copy-start.8 = (f32[128]{0:T(128)}, f32[128]{0:T(128)S(1)}, u32[]{:S(2)}) copy-start(f32[128]{0:T(128)S(1)} %add_rsqrt_fusion) | copy-start | bytes 1540
  233.7 169.9 %reduce-scatter.11.cloned.1.call-start = ((), (), s32[]{:S(2)}) async-start(), calls=%async_computation.9 | async-start | bytes 589824 | tf_op jit(solution)/shard_map/reduce_scatter | solution.py:166
  270.6 27.0 %copy-start.16 = (f32[128]{0:T(128)S(1)}, f32[128]{0:T(128)}, u32[]{:S(2)}) copy-start(f32[128]{0:T(128)} %copy-done.15) | copy-start | bytes 1540
  270.7 27.0 %copy-start.9 = (f32[128]{0:T(128)S(1)}, f32[128]{0:T(128)}, u32[]{:S(2)}) copy-start(f32[128]{0:T(128)} %copy-done.8) | copy-start | bytes 1540
  301.1 103.6 %copy-start.10 = (f32[1,256]{1,0:T(1,128)S(1)}, f32[1,256]{1,0:T(1,128)}, u32[]{:S(2)}) copy-start(f32[1,256]{1,0:T(1,128)} %get-tuple-element.474) | copy-start | bytes 3076
  301.1 103.6 %copy-start.14 = (s32[128]{0:T(128)S(1)}, s32[128]{0:T(128)}, u32[]{:S(2)}) copy-start(s32[128]{0:T(128)} %get-tuple-element.540) | copy-start | bytes 1540
  448.8 27.0 %copy-start.12 = (f32[128]{0:T(128)S(1)}, f32[128]{0:T(128)}, u32[]{:S(2)}) copy-start(f32[128]{0:T(128)} %copy-done.11) | copy-start | bytes 1540
  448.8 27.0 %copy-start.7 = (f32[128]{0:T(128)S(1)}, f32[128]{0:T(128)}, u32[]{:S(2)}) copy-start(f32[128]{0:T(128)} %copy-done.6) | copy-start | bytes 1540
Sparse Core Ops, SparseCore 0:
  26.2 35.4 reduce-scatter.4
  64.8 35.3 reduce-scatter.8
  233.8 34.2 reduce-scatter.6
  301.1 102.4 reduce-scatter.10
Sparse Core Ops, SparseCore 1:
  30.0 78.9 all-gather.2
  112.3 80.6 all-gather.4
where the time goes:
time: 485 us; the launch traced here: 484 us
  waiting for transfers between devices  281 us (58%)
  blocking collectives  108 us (22%)
  matrix products  65.6 us (14%)
  between operations  16.2 us (3%)
  other arithmetic  6.14 us (1%)
  local copies, waits for them, and re-layouts  5.38 us (1%)
    reduce_scatter x4, waiting for transfers between devices, shards(): lax.psum_scatter(partial_value.astype(jnp.bfloat16), 'mp', scatter_dimens...  151 us
    all_gather x1, waiting for transfers between devices, shards(): lax.all_gather(values, 'seq', axis=0, tiled=True)  84 us
    all_gather x1, waiting for transfers between devices, shards(): lax.all_gather(keys, 'seq', axis=0, tiled=True)  45.7 us
    psum x2, blocking collectives, shards(): squares = lax.psum(jnp.sum(state_f * state_f, axis=1), 'mp')  29.3 us
    all_gather x2, blocking collectives, shards(): lax.all_gather(flat, 'mp', axis=1, tiled=True)  26.5 us
    all_gather x2, blocking collectives, shards(): lax.all_gather(query_rows, 'mp', axis=1, tiled=True)  26.2 us
    psum x2, blocking collectives, shards(): inner = lax.psum(jnp.sum(scaled * state_f, axis=1), 'mp')  25.5 us
    dot_general x16, matrix products, backward_piece(): jnp.einsum('kqn,nkd->kqd', dscores, keys_h, preferred_element_type=jnp.fl...  25 us
  transfers between devices with their start and end apart: 6, of which 5 were waited for; matrix products, arithmetic and copies ran while one was open for 4% of the time, Pallas kernels for 0%

commit v1 on v0

v1 whole, which is shorter than its diff:
```python
import jax
import jax.numpy as jnp
from jax import lax
from jax.experimental import pallas as pl
from jax.experimental.pallas import tpu as pltpu
from jax.sharding import PartitionSpec as P

D = 4096
HD = 128
N_MP = 8
N_Y = 8
N_Z = 8
TOK = 128
ROWS = 2 * TOK
PART = D // N_MP
HEADS = 2048
TILE = HEADS // (N_Y * N_Z)
CHUNK = N_Z * TOK
epsilon = 1e-05
very_low = -1e30
LOG2E = 1.4426950408889634
SCALE = HD ** (-0.5)

MESH = pl.DeviceIdType.MESH
f32 = jnp.float32
bf16 = jnp.bfloat16
ORDER = (4, 3, 5, 2, 6, 1, 7)
NEAR = (1, 7, 2, 6, 3, 5, 4)


def dot_t(a, b):
    return lax.dot_general(a, b, (((1,), (1,)), ((), ())), preferred_element_type=f32)


def dot(a, b):
    return jnp.dot(a, b, preferred_element_type=f32)


def lane_fold(a):
    out = a[:, :128]
    for i in range(1, a.shape[1] // 128):
        out = out + a[:, i * 128 : (i + 1) * 128]
    return out


def lane_max(a):
    out = a[:, :128]
    for i in range(1, a.shape[1] // 128):
        out = jnp.maximum(out, a[:, i * 128 : (i + 1) * 128])
    return out


def row_stat(a):
    return jnp.broadcast_to(jnp.sum(lane_fold(a).T, axis=0, keepdims=True), (8, TOK))


def spread(row):
    return jnp.broadcast_to(row[0:1, :], (TOK, TOK)).T


def widen(a, times):
    return jnp.concatenate([a] * times, axis=1)


def side(a):
    return jnp.concatenate([a[:TOK], a[TOK:]], axis=1)


def stack(a):
    return jnp.concatenate([a[:, :HD], a[:, HD:]], axis=0)


def ring_units(parts, sense):
    whole = [(step, part) for step in (1, 2, 3) for part in range(parts)]
    half = range(parts // 2) if sense > 0 else range(parts // 2, parts)
    return whole + [(4, part) for part in half]


def kernel(
    x_hbm, k_hbm, v_hbm, gain_hbm, wq_hbm, wo_hbm, depth_ref, cot_hbm,
    mixed_ref, grad_ref,
    x_ref, gain_ref, wq_ref, wo_ref, cot_ref,
    kbuf, vbuf, sbuf, pbuf, best_ref,
    part_buf, part_recv, stat_buf, stat_recv,
    rows_buf, rows_recv,
    turned, tile_buf, tile_recv, mf_buf, mb_buf,
    state3,
    load_sem, first_send, first_recv,
    ring_send, ring_recv, tile_ring_send, tile_ring_recv,
    part_send_sem, part_recv_sem, stat_send_sem, stat_recv_sem, rows_send_sem, rows_recv_sem,
    tile_send_sem, tile_recv_sem,
):
    seq = lax.axis_index("seq")
    me = lax.axis_index("mp")
    y = seq // N_Z
    z = seq % N_Z
    pending = []

    def at(yy, zz, mm):
        return (yy * N_Z + zz, mm)

    loads = [
        pltpu.make_async_copy(k_hbm, kbuf.at[y, z], load_sem.at[0]),
        pltpu.make_async_copy(v_hbm, vbuf.at[y, z], load_sem.at[1]),
        pltpu.make_async_copy(x_hbm, x_ref, load_sem.at[2]),
        pltpu.make_async_copy(gain_hbm, gain_ref, load_sem.at[3]),
        pltpu.make_async_copy(wq_hbm, wq_ref, load_sem.at[4]),
        pltpu.make_async_copy(cot_hbm, cot_ref, load_sem.at[5]),
        pltpu.make_async_copy(wo_hbm, wo_ref, load_sem.at[6]),
    ]
    for load in loads:
        load.start()

    barrier = pltpu.get_barrier_semaphore()
    for k in range(1, 8):
        for target in (at(y, z, (me + k) % N_MP), at(y, (z + k) % N_Z, me), at((y + k) % N_Y, z, me)):
            pl.semaphore_signal(barrier, inc=1, device_id=target, device_id_type=MESH)
    pl.semaphore_wait(barrier, 21)

    def send(src, dst, send_sem, recv_sem, target):
        copy = pltpu.make_async_remote_copy(
            src_ref=src, dst_ref=dst, send_sem=send_sem, recv_sem=recv_sem,
            device_id=target, device_id_type=MESH,
        )
        copy.start()
        pending.append(copy)

    def arrived(dst, send_sem, recv_sem, source):
        pltpu.make_async_remote_copy(
            src_ref=dst, dst_ref=dst, send_sem=send_sem, recv_sem=recv_sem,
            device_id=source, device_id_type=MESH,
        ).wait_recv()

    def first_start(which, y_src, z_src, y_buf, z_buf):
        for k in NEAR:
            send(
                y_src, y_buf.at[y, z], first_send.at[which, 0, k], first_recv.at[which, 0, z],
                at(y, (z + k) % N_Z, me),
            )
            send(
                z_src, z_buf.at[y, z], first_send.at[which, 1, k], first_recv.at[which, 1, y],
                at((y + k) % N_Y, z, me),
            )

    def first_wait_y(which, buf, other):
        arrived(buf.at[y, other], first_send.at[which, 0, 0], first_recv.at[which, 0, other], at(y, other, me))

    def first_wait_z(which, buf, other):
        arrived(buf.at[other, z], first_send.at[which, 1, 0], first_recv.at[which, 1, other], at(other, z, me))

    targets = (at((y + 1) % N_Y, z, me), at((y + 7) % N_Y, z, me), at(y, (z + 1) % N_Z, me), at(y, (z + 7) % N_Z, me))
    sources = (targets[1], targets[0], targets[3], targets[2])

    def piece(bufs, parts, stream, unit, shift):
        sense = 1 if stream % 2 == 0 else -1
        step, part = unit
        width = 8 // parts
        turn = {4: (0, 1, 3, 2), 2: (0, 1)}[parts][part]
        if stream < 2:
            start = ((z // width + turn) % parts) * width
            return bufs[0].at[(y + 8 - sense * (step - shift)) % N_Y, pl.ds(start, width)]
        start = ((y // width + turn) % parts) * width
        return bufs[1].at[pl.ds(start, width), (z + 8 - sense * (step - shift)) % N_Z]

    def ring_start(bufs, parts, sems, stream, unit):
        index = ring_units(parts, 1 if stream % 2 == 0 else -1).index(unit)
        ref = piece(bufs, parts, stream, unit, 1)
        send(ref, ref, sems[0].at[stream, index], sems[1].at[stream, index], targets[stream])

    def ring_turn(bufs, parts, sems, index):
        for stream in range(4):
            units = ring_units(parts, 1 if stream % 2 == 0 else -1)
            step, part = units[index]
            ref = piece(bufs, parts, stream, (step, part), 0)
            arrived(ref, sems[0].at[stream, index], sems[1].at[stream, index], sources[stream])
            if (step + 1, part) in units:
                ring_start(bufs, parts, sems, stream, (step + 1, part))

    kv = (kbuf, vbuf)
    kv_sems = (ring_send, ring_recv)
    tiles = (mf_buf, mb_buf)
    tile_sems = (tile_ring_send, tile_ring_recv)

    def kv_inject(part):
        turn = (0, 1, 3, 2)[part]
        if part == 0:
            loads[0].wait()
            loads[1].wait()
            first_wait_y(0, kbuf, z + 1 - 2 * (z % 2))
            first_wait_z(0, vbuf, y + 1 - 2 * (y % 2))
        else:
            for i in range(2):
                first_wait_y(0, kbuf, ((z // 2 + turn) % 4) * 2 + i)
                first_wait_z(0, vbuf, ((y // 2 + turn) % 4) * 2 + i)
        for stream in range(4):
            ring_start(kv, 4, kv_sems, stream, (1, part))

    def part_send(which, peer, k):
        send(
            part_buf.at[which, pl.ds(pl.multiple_of(peer * ROWS, ROWS), ROWS)],
            part_recv.at[which, me],
            part_send_sem.at[which, k], part_recv_sem.at[which, me], at(y, z, peer),
        )

    def part_sum(which):
        total = part_buf[which, pl.ds(pl.multiple_of(me * ROWS, ROWS), ROWS)].astype(f32)
        for k in ORDER:
            peer = (me + k) % N_MP
            arrived(part_recv.at[which, peer], part_send_sem.at[which, 0], part_recv_sem.at[which, peer], at(y, z, peer))
            total = total + part_recv[which, peer].astype(f32)
        return total

    def stat_start(which, row):
        stat_buf[which] = row
        for k in ORDER:
            peer = (me + k) % N_MP
            send(
                stat_buf.at[which], stat_recv.at[which, me],
                stat_send_sem.at[which, k], stat_recv_sem.at[which, me], at(y, z, peer),
            )

    def stat_sum(which):
        total = stat_buf[which]
        for k in ORDER:
            peer = (me + k) % N_MP
            arrived(stat_recv.at[which, peer], stat_send_sem.at[which, 0], stat_recv_sem.at[which, peer], at(y, z, peer))
            total = total + stat_recv[which, peer]
        return total

    def rows_start(which, rows):
        rows_buf[which] = rows
        rows_recv[which, me] = rows
        for k in ORDER:
            peer = (me + k) % N_MP
            send(
                rows_buf.at[which], rows_recv.at[which, me],
                rows_send_sem.at[which, k], rows_recv_sem.at[which, me], at(y, z, peer),
            )

    def rows_wait(which):
        for k in NEAR:
            peer = (me + k) % N_MP
            arrived(rows_recv.at[which, peer], rows_send_sem.at[which, 0], rows_recv_sem.at[which, peer], at(y, z, peer))

    def project(which, product):
        for k in ORDER + (0,):
            peer = (me + k) % N_MP
            cols = product(pl.ds(pl.multiple_of(peer * 256, 256), 256)).astype(bf16)
            part_buf[which, pl.ds(pl.multiple_of(peer * ROWS, ROWS), ROWS)] = stack(cols)
            if k:
                part_send(which, peer, k)

    def project_query(which, state_f):
        scaled = (state_f * gain_ref[...]).astype(bf16)
        project(which, lambda cols: dot(scaled, wq_ref[:, cols]))

    def project_grad(which, rows):
        project(which, lambda cols: dot_t(rows, wo_ref[cols, :]))

    live2 = jnp.where(depth_ref[0] >= 2, 1.0, 0.0).astype(f32)
    live3 = jnp.where(depth_ref[0] >= 3, 1.0, 0.0).astype(f32)

    def keys_at(c):
        return kbuf[c].reshape(CHUNK, HD)

    def values_at(c):
        return vbuf[c].reshape(CHUNK, HD)

    shape = (ROWS, CHUNK)

    def scores(query, c):
        s = dot_t(query, keys_at(c))
        sbuf[c] = s
        best_ref[...] = jnp.maximum(best_ref[...], lane_max(s))

    def own_scores(query):
        s = dot_t(query, keys_at(y))
        token = lax.broadcasted_iota(jnp.int32, shape, 0) % TOK + z * TOK
        s = jnp.where(lax.broadcasted_iota(jnp.int32, shape, 1) <= token, s, very_low)
        sbuf[y] = s
        best_ref[...] = lane_max(s)

    def step_scores(query, step):
        @pl.when(y >= step)
        def _():
            scores(query, y - step)

        if step < 4:
            @pl.when(y + step >= N_Y)
            def _():
                scores(query, y + step - N_Y)

    def weigh(level, factor):
        best = jnp.max(best_ref[...], axis=1, keepdims=True)
        if factor is not None:
            best = best * factor

        def turn(c, carry):
            total, accum = carry
            s = sbuf[c]
            if factor is not None:
                s = s * factor
            p = jnp.exp2(s - best)
            total = total + lane_fold(p)
            p = p.astype(bf16)
            pbuf[level, c] = p
            return total, accum + dot(p, values_at(c))

        total, accum = lax.fori_loop(
            0, y + 1, turn, (jnp.zeros((ROWS, 128), f32), jnp.zeros((ROWS, HD), f32))
        )
        share = 1.0 / jnp.sum(total, axis=1, keepdims=True)
        return (accum * share).astype(bf16), share

    def backward(level, grad_att, attended, share):
        delta = jnp.sum(grad_att.astype(f32) * attended.astype(f32), axis=1, keepdims=True)

        def turn(c, accum):
            dprobs = dot_t(grad_att, values_at(c))
            ds = (pbuf[level, c].astype(f32) * (dprobs - delta)).astype(bf16)
            return accum + dot(ds, keys_at(c))

        accum = lax.fori_loop(0, y + 1, turn, jnp.zeros((ROWS, HD), f32))
        return (accum * (share * SCALE)).astype(bf16)

    def rows_product(which, weight):
        total = dot(rows_recv[which, 0], weight(0))
        for h in range(1, N_MP):
            total = total + dot(rows_recv[which, h], weight(h))
        return total

    def out_product(which):
        return rows_product(which, lambda h: wo_ref[h * 256 : (h + 1) * 256, :])

    def tile_product(which, buf):
        return rows_product(which, lambda h: buf[h].reshape(256, 256))

    def query_product(which):
        total = dot_t(rows_recv[which, 0], wq_ref[:, 0:256])
        for h in range(1, N_MP):
            total = total + dot_t(rows_recv[which, h], wq_ref[:, h * 256 : (h + 1) * 256])
        return total

    def inverse_of(which):
        return lax.rsqrt(stat_sum(which) * (1.0 / D) + epsilon)

    def twice(a):
        return jnp.concatenate([a, a], axis=0)

    first_start(0, k_hbm, v_hbm, kbuf, vbuf)
    for load in loads[2:5]:
        load.wait()
    x_f = x_ref[...].astype(f32)
    project_query(0, x_f)
    stat_start(0, row_stat(x_f * x_f))
    kv_inject(0)
    kv_inject(1)
    for load in loads[5:]:
        load.wait()
    project_grad(1, cot_ref[...])
    kv_inject(2)
    kv_inject(3)

    gain = gain_ref[...]
    tile_f = dot((wo_ref[pl.ds(pl.multiple_of(seq * TILE, TILE), TILE), :].astype(f32) * gain).astype(bf16), wq_ref[...])
    group = wq_ref[:, pl.ds(pl.multiple_of(seq // 4 * 128, 128), 128)]
    turned[...] = (group.astype(f32).T * gain).astype(bf16)
    tile_b = dot_t(turned[pl.ds(pl.multiple_of(seq % 4 * TILE, TILE), TILE), :], wo_ref[...])
    for h in range(N_MP):
        tile_buf[h, 0] = tile_f[:, h * 256 : (h + 1) * 256].astype(bf16)
        tile_buf[h, 1] = tile_b[:, h * 256 : (h + 1) * 256].astype(bf16)
    for k in ORDER:
        peer = (me + k) % N_MP
        send(tile_buf.at[peer], tile_recv.at[me], tile_send_sem.at[k], tile_recv_sem.at[me], at(y, z, peer))

    ring_turn(kv, 4, kv_sems, 0)
    ring_turn(kv, 4, kv_sems, 1)
    raw2 = part_sum(0)
    inverse2 = inverse_of(0)
    query2 = (raw2 * (twice(spread(inverse2)) * (SCALE * LOG2E))).astype(bf16)
    own_scores(query2)
    ring_turn(kv, 4, kv_sems, 2)
    ring_turn(kv, 4, kv_sems, 3)
    step_scores(query2, 1)
    ring_turn(kv, 4, kv_sems, 4)
    ring_turn(kv, 4, kv_sems, 5)
    tile = tile_buf[me].astype(f32)
    for k in ORDER:
        peer = (me + k) % N_MP
        arrived(tile_recv.at[peer], tile_send_sem.at[0], tile_recv_sem.at[peer], at(y, z, peer))
        tile = tile + tile_recv[peer].astype(f32)
    mf_buf[y, z] = tile[0].astype(bf16)
    mb_buf[y, z] = tile[1].astype(bf16)
    first_start(1, mf_buf.at[y, z], mb_buf.at[y, z], mf_buf, mb_buf)
    ring_turn(kv, 4, kv_sems, 6)
    ring_turn(kv, 4, kv_sems, 7)
    step_scores(query2, 2)
    for index in range(8, 12):
        ring_turn(kv, 4, kv_sems, index)
    for k in NEAR:
        first_wait_y(1, mf_buf, (z + k) % N_Z)
        first_wait_z(1, mb_buf, (y + k) % N_Y)
    for part in range(2):
        for stream in range(4):
            ring_start(tiles, 2, tile_sems, stream, (1, part))
    step_scores(query2, 3)
    ring_turn(kv, 4, kv_sems, 12)
    ring_turn(kv, 4, kv_sems, 13)
    step_scores(query2, 4)

    attended2, share2 = weigh(0, None)
    rows_start(0, side(attended2))
    for index in range(7):
        ring_turn(tiles, 2, tile_sems, index)
        if index == 3:
            grad_att3 = part_sum(1)
    rows_wait(0)
    x3 = (x_ref[...].astype(f32) + live2 * out_product(0)).astype(bf16)
    state3[...] = x3
    x3_f = x3.astype(f32)
    stat_start(1, row_stat(x3_f * x3_f))

    raw3 = raw2 + stack(live2 * tile_product(0, mf_buf))
    query3 = (raw3 * (SCALE * LOG2E)).astype(bf16)
    own_scores(query3)

    def score_turn(c, carry):
        scores(query3, c)
        return carry

    lax.fori_loop(0, y, score_turn, 0)
    project_grad(2, x3)
    inverse3 = inverse_of(1)
    factor3 = twice(spread(inverse3))[:, :1]
    attended3, share3 = weigh(1, factor3)
    rows_start(1, side(attended3))
    grad_query3 = backward(1, (grad_att3 * live3).astype(bf16), attended3, share3)
    rows_start(2, side(grad_query3))
    stat_start(2, row_stat(side(grad_query3.astype(f32) * raw3)))

    rows_wait(1)
    mixed_ref[...] = (state3[...].astype(f32) + live3 * out_product(1)).astype(bf16)

    state_part = part_sum(2)
    inner3 = stat_sum(2)
    coef3 = inverse3 * inverse3 * inverse3 * inner3 * (1.0 / D)
    rows_wait(2)
    through = stack(tile_product(2, mb_buf))
    grad_att2 = live2 * (grad_att3 + twice(spread(inverse3)) * through - twice(spread(coef3)) * state_part)
    grad_query2 = backward(0, grad_att2.astype(bf16), attended2, share2)
    rows_start(3, side(grad_query2))
    stat_start(3, row_stat(side(grad_query2.astype(f32) * raw2)))

    def grad_input(which, state, inverse, coef, grad_f):
        scaled = query_product(which) * gain_ref[...]
        inv = widen(spread(inverse), PART // 128)
        return (grad_f + inv * scaled - state.astype(f32) * widen(spread(coef), PART // 128)).astype(bf16)

    grad3 = grad_input(2, state3[...], inverse3, coef3, cot_ref[...].astype(f32))
    inner2 = stat_sum(3)
    coef2 = inverse2 * inverse2 * inverse2 * inner2 * (1.0 / D)
    rows_wait(3)
    grad_ref[...] = grad_input(3, x_ref[...], inverse2, coef2, grad3.astype(f32))

    for copy in pending:
        copy.wait_send()


def shards(hidden, keys, values, norm_gain, w_query, w_out, depth, cotangent):
    any_spec = pl.BlockSpec(memory_space=pl.ANY)
    vmem_spec = pl.BlockSpec(memory_space=pltpu.VMEM)
    sem = pltpu.SemaphoreType.DMA
    out = jax.ShapeDtypeStruct((TOK, PART), bf16)
    return pl.pallas_call(
        kernel,
        out_shape=(out, out),
        in_specs=[any_spec] * 6 + [pl.BlockSpec(memory_space=pltpu.SMEM), any_spec],
        out_specs=(vmem_spec, vmem_spec),
        scratch_shapes=[
            pltpu.VMEM((TOK, PART), bf16),
            pltpu.VMEM((1, PART), f32),
            pltpu.VMEM((PART, HEADS), bf16),
            pltpu.VMEM((HEADS, PART), bf16),
            pltpu.VMEM((TOK, PART), bf16),
            pltpu.VMEM((N_Y, N_Z, TOK, HD), bf16),
            pltpu.VMEM((N_Y, N_Z, TOK, HD), bf16),
            pltpu.VMEM((N_Y, ROWS, CHUNK), f32),
            pltpu.VMEM((2, N_Y, ROWS, CHUNK), bf16),
            pltpu.VMEM((ROWS, 128), f32),
            pltpu.VMEM((3, HEADS, HD), bf16),
            pltpu.VMEM((3, N_MP, ROWS, HD), bf16),
            pltpu.VMEM((4, 8, TOK), f32),
            pltpu.VMEM((4, N_MP, 8, TOK), f32),
            pltpu.VMEM((4, TOK, ROWS), bf16),
            pltpu.VMEM((4, N_MP, TOK, ROWS), bf16),
            pltpu.VMEM((128, PART), bf16),
            pltpu.VMEM((N_MP, 2, TILE, ROWS), bf16),
            pltpu.VMEM((N_MP, 2, TILE, ROWS), bf16),
            pltpu.VMEM((N_Y, N_Z, TILE, ROWS), bf16),
            pltpu.VMEM((N_Y, N_Z, TILE, ROWS), bf16),
            pltpu.VMEM((TOK, PART), bf16),
            sem((7,)),
            sem((2, 2, 8)), sem((2, 2, 8)),
            sem((4, 14)), sem((4, 14)), sem((4, 7)), sem((4, 7)),
            sem((3, 8)), sem((3, 8)), sem((4, 8)), sem((4, 8)), sem((4, 8)), sem((4, 8)),
            sem((8,)), sem((8,)),
        ],
        compiler_params=pltpu.CompilerParams(
            collective_id=0, has_side_effects=True, vmem_limit_bytes=60 * 1024 * 1024
        ),
        name="recursion",
    )(hidden, keys, values, norm_gain.reshape(1, PART), w_query, w_out, depth, cotangent)


def solution(mesh):
    return jax.shard_map(
        shards,
        mesh=mesh,
        in_specs=(
            P("seq", "mp"),
            P("seq", "mp"),
            P("seq", "mp"),
            P("mp"),
            P("mp", None),
            P(None, "mp"),
            P("seq"),
            P("seq", "mp"),
        ),
        out_specs=(P("seq", "mp"), P("seq", "mp")),
        check_vma=False,
    )
```

time: 485 us -> 107 us (0.22)
  the two profiles are of different devices: /device:TPU:312 before, /device:TPU:57 now
where the time goes in v1:
time: 107 us
  Pallas kernels  103 us (96%)
  local copies, waits for them, and re-layouts  3.14 us (3%)
  between operations  1.29 us (1%)
    pallas_call x1, Pallas kernels, shards(): pl.pallas_call(kernel, out_shape=(out, out), in_specs=[any_spec] * 6 + [p...  103 us
    unnamed x2, local copies, waits for them, and re-layouts  3.14 us

profile of v1, /device:TPU:57, one launch (start us, length us, event | category | flops | bytes accessed | tf_op | source)
XLA Modules:
  0.0 107.0 jit_solution(17214330275036894056)
XLA Ops:
  1.3 102.5 %recursion.1 = (bf16[128,512]{1,0:T(8,128)(2,1)}, bf16[128,512]{1,0:T(8,128)(2,1)}) custom-call(bf16[128,512]{1,0:T(8,128)(2,1)} %x_hbm.1, bf16[128,128]{1,0:T(8,128)(2,1)} %k_hbm.1, bf16[128,128]{1,0:T(8,128)(2,1)} %v_hbm.1, f32[1,512]{1,0:T(1,128)} %bitcast.1, bf16[512,2048]{1,0:T(8,128)(2,1)} %wq_hbm.1, bf16[2048,512]{1,0:T(8,128)(2,1)} %wo_hbm.1, ...), custom_call_target="tpu_custom_call" | custom-call | tf_op jit(solution)/shard_map/recursion/pallas_call | solution.py:474
  103.8 1.6 %copy.13 = bf16[128,512]{1,0:T(8,128)(2,1)} copy(bf16[128,512]{1,0:T(8,128)(2,1)} %get-tuple-element.4) | data formatting | bytes 262144
  105.4 1.6 %copy.14 = bf16[128,512]{1,0:T(8,128)(2,1)} copy(bf16[128,512]{1,0:T(8,128)(2,1)} %get-tuple-element.5) | data formatting | bytes 262144

commit v2 on v1

v2 whole, which is shorter than its diff:
```python
import jax
import jax.numpy as jnp
from jax import lax
from jax.experimental import pallas as pl
from jax.experimental.pallas import tpu as pltpu
from jax.sharding import PartitionSpec as P

D = 4096
HD = 128
N_MP = 8
N_Y = 8
N_Z = 8
TOK = 128
ROWS = 2 * TOK
PART = D // N_MP
HEADS = 2048
TILE = HEADS // (N_Y * N_Z)
CHUNK = N_Z * TOK
epsilon = 1e-05
very_low = -1e30
LOG2E = 1.4426950408889634
SCALE = HD ** (-0.5)

MESH = pl.DeviceIdType.MESH
f32 = jnp.float32
bf16 = jnp.bfloat16
ORDER = (4, 3, 5, 2, 6, 1, 7)
NEAR = (1, 7, 2, 6, 3, 5, 4)


def dot_t(a, b):
    return lax.dot_general(a, b, (((1,), (1,)), ((), ())), preferred_element_type=f32)


def dot(a, b):
    return jnp.dot(a, b, preferred_element_type=f32)


def lane_fold(a):
    out = a[:, :128]
    for i in range(1, a.shape[1] // 128):
        out = out + a[:, i * 128 : (i + 1) * 128]
    return out


def lane_max(a):
    out = a[:, :128]
    for i in range(1, a.shape[1] // 128):
        out = jnp.maximum(out, a[:, i * 128 : (i + 1) * 128])
    return out


def row_stat(a):
    return jnp.broadcast_to(jnp.sum(lane_fold(a).T, axis=0, keepdims=True), (8, TOK))


def spread(row):
    return jnp.broadcast_to(row[0:1, :], (TOK, TOK)).T


def widen(a, times):
    return jnp.concatenate([a] * times, axis=1)


def side(a):
    return jnp.concatenate([a[:TOK], a[TOK:]], axis=1)


def stack(a):
    return jnp.concatenate([a[:, :HD], a[:, HD:]], axis=0)


def ring_units(parts, sense):
    whole = [(step, part) for step in (1, 2, 3) for part in range(parts)]
    half = range(parts // 2) if sense > 0 else range(parts // 2, parts)
    return whole + [(4, part) for part in half]


def kernel(
    x_hbm, k_hbm, v_hbm, gain_hbm, wq_hbm, wo_hbm, depth_ref, cot_hbm,
    mixed_ref, grad_ref,
    x_ref, gain_ref, wq_ref, wo_ref, cot_ref,
    kbuf, vbuf, sbuf, pbuf, best_ref,
    part_buf, part_recv, stat_buf, stat_recv,
    rows_recv,
    turned, tile_buf, tile_recv, tiles,
    state3,
    load_sem, first_send, first_recv,
    ring_send, ring_recv, tile_ring_send, tile_ring_recv,
    part_send_sem, part_recv_sem, stat_send_sem, stat_recv_sem, rows_send_sem, rows_recv_sem,
    tile_send_sem, tile_recv_sem,
):
    seq = lax.axis_index("seq")
    me = lax.axis_index("mp")
    y = seq // N_Z
    z = seq % N_Z
    pending = []

    def at(yy, zz, mm):
        return (yy * N_Z + zz, mm)

    loads = [
        pltpu.make_async_copy(k_hbm, kbuf.at[y, z], load_sem.at[0]),
        pltpu.make_async_copy(v_hbm, vbuf.at[y, z], load_sem.at[1]),
        pltpu.make_async_copy(x_hbm, x_ref, load_sem.at[2]),
        pltpu.make_async_copy(gain_hbm, gain_ref, load_sem.at[3]),
        pltpu.make_async_copy(wq_hbm, wq_ref, load_sem.at[4]),
        pltpu.make_async_copy(cot_hbm, cot_ref, load_sem.at[5]),
        pltpu.make_async_copy(wo_hbm, wo_ref, load_sem.at[6]),
    ]
    for load in loads:
        load.start()

    targets = (at(y, (z + 1) % N_Z, me), at(y, (z + 7) % N_Z, me), at((y + 1) % N_Y, z, me), at((y + 7) % N_Y, z, me))
    barrier = pltpu.get_barrier_semaphore()
    for target in targets + tuple(at(y, z, (me + k) % N_MP) for k in range(1, 8)):
        pl.semaphore_signal(barrier, inc=1, device_id=target, device_id_type=MESH)
    pl.semaphore_wait(barrier, 11)

    def send(src, dst, send_sem, recv_sem, target):
        copy = pltpu.make_async_remote_copy(
            src_ref=src, dst_ref=dst, send_sem=send_sem, recv_sem=recv_sem,
            device_id=target, device_id_type=MESH,
        )
        copy.start()
        pending.append(copy)

    def arrived(dst, send_sem, recv_sem, source):
        pltpu.make_async_remote_copy(
            src_ref=dst, dst_ref=dst, send_sem=send_sem, recv_sem=recv_sem,
            device_id=source, device_id_type=MESH,
        ).wait_recv()

    def first_piece(gather, stream, step, shift):
        bufs = gather[0]
        away = (1 if stream % 2 == 0 else -1) * (step - shift)
        if stream < 2:
            block = bufs[0].at[y, (z + 8 - away) % N_Z]
        else:
            block = bufs[1].at[(y + 8 - away) % N_Y, z]
        if step < 4:
            return block
        half = bufs[0].shape[2] // 2
        return block.at[pl.ds(stream % 2 * half, half)]

    def first_start(gather, step):
        for stream in range(4):
            ref = first_piece(gather, stream, step, 1)
            send(ref, ref, gather[2].at[stream, step], gather[3].at[stream, step], targets[stream])

    def first_turn(gather, step):
        for stream in range(4):
            ref = first_piece(gather, stream, step, 0)
            arrived(ref, gather[2].at[stream, step], gather[3].at[stream, step], targets[stream ^ 1])
        if step < 4:
            first_start(gather, step + 1)

    def piece(gather, stream, unit, shift):
        bufs, parts = gather[0], gather[1]
        away = (1 if stream % 2 == 0 else -1) * (unit[0] - shift)
        width = 8 // parts
        mine, across = (z, y) if stream < 2 else (y, z)
        if parts == 4:
            toward = 2 * (mine % 2) - 1
            turn = (0, toward, -toward, 2)[unit[1]]
        else:
            turn = unit[1]
        span = pl.ds((mine // width + parts + turn) % parts * width, width)
        if stream < 2:
            return bufs[0].at[(across + 8 - away) % N_Y, span]
        return bufs[1].at[span, (across + 8 - away) % N_Z]

    def ring_start(gather, stream, unit):
        index = ring_units(gather[1], 1 if stream % 2 == 0 else -1).index(unit)
        ref = piece(gather, stream, unit, 1)
        send(ref, ref, gather[4].at[stream, index], gather[5].at[stream, index], targets[stream ^ 2])

    def inject(gather, part):
        for stream in range(4):
            ring_start(gather, stream, (1, part))

    def ring_turn(gather, index):
        for stream in range(4):
            units = ring_units(gather[1], 1 if stream % 2 == 0 else -1)
            step, part = units[index]
            ref = piece(gather, stream, (step, part), 0)
            arrived(ref, gather[4].at[stream, index], gather[5].at[stream, index], targets[stream ^ 3])
            if (step + 1, part) in units:
                ring_start(gather, stream, (step + 1, part))

    kv = ((kbuf, vbuf), 4, first_send.at[0], first_recv.at[0], ring_send, ring_recv)
    tile_f = ((tiles.at[0], tiles.at[1]), 2, first_send.at[1], first_recv.at[1], tile_ring_send.at[0], tile_ring_recv.at[0])
    tile_b = ((tiles.at[2], tiles.at[3]), 2, first_send.at[2], first_recv.at[2], tile_ring_send.at[1], tile_ring_recv.at[1])

    def part_send(which, peer, k):
        send(
            part_buf.at[which, pl.ds(pl.multiple_of(peer * ROWS, ROWS), ROWS)],
            part_recv.at[which, me],
            part_send_sem.at[which, k], part_recv_sem.at[which, me], at(y, z, peer),
        )

    def part_sum(which):
        total = part_buf[which, pl.ds(pl.multiple_of(me * ROWS, ROWS), ROWS)].astype(f32)
        for k in ORDER:
            peer = (me + k) % N_MP
            arrived(part_recv.at[which, peer], part_send_sem.at[which, 0], part_recv_sem.at[which, peer], at(y, z, peer))
            total = total + part_recv[which, peer].astype(f32)
        return total

    def stat_start(which, row):
        stat_buf[which] = row
        for k in ORDER:
            peer = (me + k) % N_MP
            send(
                stat_buf.at[which], stat_recv.at[which, me],
                stat_send_sem.at[which, k], stat_recv_sem.at[which, me], at(y, z, peer),
            )

    def stat_sum(which):
        total = stat_buf[which]
        for k in ORDER:
            peer = (me + k) % N_MP
            arrived(stat_recv.at[which, peer], stat_send_sem.at[which, 0], stat_recv_sem.at[which, peer], at(y, z, peer))
            total = total + stat_recv[which, peer]
        return total

    sibling = me + 1 - 2 * (me % 2)

    def rows_send(which, src, k, slot, target):
        send(
            src, rows_recv.at[which, slot], rows_send_sem.at[which, k], rows_recv_sem.at[which, slot], at(y, z, target)
        )

    def rows_start(which, rows):
        rows_recv[which, me] = rows
        for k in (4, 2, 6):
            rows_send(which, rows_recv.at[which, me], k, me, (me + k) % N_MP)
        rows_send(which, rows_recv.at[which, me], 0, me, sibling)

    def rows_wait(which, source):
        arrived(
            rows_recv.at[which, source], rows_send_sem.at[which, 0], rows_recv_sem.at[which, source], at(y, z, source)
        )

    def rows_forward(which):
        for k in (2, 6, 4):
            source = (me + k) % N_MP
            rows_wait(which, source)
            rows_send(which, rows_recv.at[which, source], k + 1, source, sibling)

    def rows_product(which, product, wait=True):
        total = product(rows_recv[which, me], me)
        for k in (2, 6, 4):
            source = (me + k) % N_MP
            total = total + product(rows_recv[which, source], source)
        for k in (0, 2, 6, 4):
            source = (sibling + k) % N_MP
            if wait:
                rows_wait(which, source)
            total = total + product(rows_recv[which, source], source)
        return total

    def drain():
        for copy in pending:
            copy.wait_send()
        pending.clear()

    def project(which, product, peers=ORDER + (0,)):
        for k in peers:
            peer = (me + k) % N_MP
            cols = product(pl.ds(pl.multiple_of(peer * 256, 256), 256)).astype(bf16)
            part_buf[which, pl.ds(pl.multiple_of(peer * ROWS, ROWS), ROWS)] = stack(cols)
            if k:
                part_send(which, peer, k)

    def query_cols(rows):
        return lambda cols: dot(rows, wq_ref[:, cols])

    def grad_cols(rows):
        return lambda cols: dot_t(rows, wo_ref[cols, :])

    live2 = jnp.where(depth_ref[0] >= 2, 1.0, 0.0).astype(f32)
    live3 = jnp.where(depth_ref[0] >= 3, 1.0, 0.0).astype(f32)

    def keys_at(c):
        return kbuf[c].reshape(CHUNK, HD)

    def values_at(c):
        return vbuf[c].reshape(CHUNK, HD)

    shape = (ROWS, CHUNK)

    def scores(query, c):
        s = dot_t(query, keys_at(c))
        sbuf[c] = s
        best_ref[...] = jnp.maximum(best_ref[...], lane_max(s))

    def own_scores(query):
        s = dot_t(query, keys_at(y))
        token = lax.broadcasted_iota(jnp.int32, shape, 0) % TOK + z * TOK
        s = jnp.where(lax.broadcasted_iota(jnp.int32, shape, 1) <= token, s, very_low)
        sbuf[y] = s
        best_ref[...] = lane_max(s)

    def step_scores(query, step):
        @pl.when(y >= step)
        def _():
            scores(query, y - step)

        if step < 4:
            @pl.when(y + step >= N_Y)
            def _():
                scores(query, y + step - N_Y)

    def weigh(level, factor):
        best = jnp.max(best_ref[...], axis=1, keepdims=True)
        if factor is not None:
            best = best * factor

        def weights(c):
            s = sbuf[c]
            if factor is not None:
                s = s * factor
            p = jnp.exp2(s - best)
            total = lane_fold(p)
            p = p.astype(bf16)
            pbuf[level, c] = p
            return total, dot(p, values_at(c))

        def two(i, carry):
            first, second = weights(2 * i), weights(2 * i + 1)
            return carry[0] + first[0] + second[0], carry[1] + first[1] + second[1]

        def one(c, carry):
            first = weights(c)
            return carry[0] + first[0], carry[1] + first[1]

        count = y + 1
        carry = lax.fori_loop(0, count // 2, two, (jnp.zeros((ROWS, 128), f32), jnp.zeros((ROWS, HD), f32)))
        total, accum = lax.fori_loop(count // 2 * 2, count, one, carry)
        share = 1.0 / jnp.sum(total, axis=1, keepdims=True)
        return (accum * share).astype(bf16), share

    def backward(level, grad_att, attended, share):
        delta = jnp.sum(grad_att.astype(f32) * attended.astype(f32), axis=1, keepdims=True)

        def turn(c, accum):
            dprobs = dot_t(grad_att, values_at(c))
            ds = (pbuf[level, c].astype(f32) * (dprobs - delta)).astype(bf16)
            return accum + dot(ds, keys_at(c))

        accum = lax.fori_loop(0, y + 1, turn, jnp.zeros((ROWS, HD), f32))
        return (accum * (share * SCALE)).astype(bf16)

    def head_cols(j):
        return pl.ds(pl.multiple_of(j * ROWS, ROWS), ROWS)

    def out_product(rows, j):
        return dot(rows, wo_ref[head_cols(j), :])

    def query_product(rows, j):
        return dot_t(rows, wq_ref[:, head_cols(j)])

    def tile_product(first):
        def product(rows, j):
            return jnp.concatenate(
                [dot(rows, tiles[first + half, j].reshape(ROWS, HD)) for half in range(2)], axis=0
            )
        return product

    def inverse_of(which):
        return lax.rsqrt(stat_sum(which) * (1.0 / D) + epsilon)

    def twice(a):
        return jnp.concatenate([a, a], axis=0)

    loads[0].wait()
    loads[1].wait()
    first_start(kv, 1)
    for load in loads[2:5]:
        load.wait()
    x_f = x_ref[...].astype(f32)
    gain = gain_ref[...]
    project(0, query_cols((x_f * gain).astype(bf16)))
    stat_start(0, row_stat(x_f * x_f))
    first_turn(kv, 1)
    inject(kv, 0)
    for load in loads[5:]:
        load.wait()
    cot = cot_ref[...]
    project(1, grad_cols(cot), ORDER[:3])
    first_turn(kv, 2)
    inject(kv, 1)
    project(1, grad_cols(cot), ORDER[3:] + (0,))
    first_turn(kv, 3)
    inject(kv, 2)
    rows_f = dot((wo_ref[pl.ds(pl.multiple_of(seq * TILE, TILE), TILE), :].astype(f32) * gain).astype(bf16), wq_ref[...])
    ring_turn(kv, 0)
    first_turn(kv, 4)
    inject(kv, 3)
    group = wq_ref[:, pl.ds(pl.multiple_of(seq // 4 * 128, 128), 128)]
    turned[...] = (group.astype(f32).T * gain).astype(bf16)
    rows_b = dot_t(turned[pl.ds(pl.multiple_of(seq % 4 * TILE, TILE), TILE), :], wo_ref[...])
    ring_turn(kv, 1)
    for h in range(N_MP):
        for i, rows in enumerate((rows_f, rows_b)):
            for half in range(2):
                start = h * ROWS + half * HD
                tile_buf[h, 2 * i + half] = rows[:, start : start + HD].astype(bf16)
    for k in ORDER:
        peer = (me + k) % N_MP
        send(tile_buf.at[peer], tile_recv.at[me], tile_send_sem.at[k], tile_recv_sem.at[me], at(y, z, peer))
    ring_turn(kv, 2)
    raw2 = part_sum(0)
    inverse2 = inverse_of(0)
    query2 = (raw2 * (twice(spread(inverse2)) * (SCALE * LOG2E))).astype(bf16)
    ring_turn(kv, 3)
    own_scores(query2)
    ring_turn(kv, 4)
    step_scores(query2, 1)
    ring_turn(kv, 5)
    tile = tile_buf[me].astype(f32)
    for k in ORDER:
        peer = (me + k) % N_MP
        arrived(tile_recv.at[peer], tile_send_sem.at[0], tile_recv_sem.at[peer], at(y, z, peer))
        tile = tile + tile_recv[peer].astype(f32)
    for i in range(4):
        tiles[i, y, z] = tile[i].astype(bf16)
    first_start(tile_f, 1)
    ring_turn(kv, 6)
    grad_att3 = part_sum(1)
    ring_turn(kv, 7)
    first_turn(tile_f, 1)
    first_start(tile_b, 1)
    step_scores(query2, 2)
    ring_turn(kv, 8)
    first_turn(tile_f, 2)
    ring_turn(kv, 9)
    first_turn(tile_b, 1)
    ring_turn(kv, 10)
    first_turn(tile_f, 3)
    inject(tile_f, 0)
    ring_turn(kv, 11)
    first_turn(tile_f, 4)
    inject(tile_f, 1)
    step_scores(query2, 3)
    ring_turn(kv, 12)
    ring_turn(kv, 13)
    step_scores(query2, 4)

    ring_turn(tile_f, 0)
    ring_turn(tile_f, 1)
    attended2, share2 = weigh(0, None)
    rows_start(0, side(attended2))
    ring_turn(tile_f, 2)
    ring_turn(tile_f, 3)
    first_turn(tile_b, 2)
    drain()
    rows_forward(0)
    ring_turn(tile_f, 4)
    first_turn(tile_b, 3)
    inject(tile_b, 0)
    x3 = (x_ref[...].astype(f32) + live2 * rows_product(0, out_product)).astype(bf16)
    state3[...] = x3
    x3_f = x3.astype(f32)
    stat_start(1, row_stat(x3_f * x3_f))

    project(2, grad_cols(x3))
    first_turn(tile_b, 4)
    inject(tile_b, 1)
    ring_turn(tile_f, 5)
    ring_turn(tile_f, 6)
    raw3 = raw2 + live2 * rows_product(0, tile_product(0), wait=False)
    query3 = (raw3 * (SCALE * LOG2E)).astype(bf16)
    own_scores(query3)

    def score_turn(c, carry):
        scores(query3, c)
        return carry

    lax.fori_loop(0, y, score_turn, 0)
    ring_turn(tile_b, 0)
    ring_turn(tile_b, 1)
    inverse3 = inverse_of(1)
    factor3 = twice(spread(inverse3))[:, :1]
    attended3, share3 = weigh(1, factor3)
    ring_turn(tile_b, 2)
    ring_turn(tile_b, 3)
    grad_query3 = backward(1, (grad_att3 * live3).astype(bf16), attended3, share3)
    rows_start(2, side(grad_query3))
    stat_start(2, row_stat(side(grad_query3.astype(f32) * raw3)))
    ring_turn(tile_b, 4)
    ring_turn(tile_b, 5)
    drain()
    rows_forward(2)
    ring_turn(tile_b, 6)
    state_part = part_sum(2)

    through = rows_product(2, tile_product(2))
    inner3 = stat_sum(2)
    coef3 = inverse3 * inverse3 * inverse3 * inner3 * (1.0 / D)
    grad_att2 = live2 * (grad_att3 + twice(spread(inverse3)) * through - twice(spread(coef3)) * state_part)
    rows_start(1, side(attended3))
    grad_query2 = backward(0, grad_att2.astype(bf16), attended2, share2)
    rows_start(3, side(grad_query2))
    stat_start(3, row_stat(side(grad_query2.astype(f32) * raw2)))
    rows_forward(1)
    mixed_ref[...] = (state3[...].astype(f32) + live3 * rows_product(1, out_product)).astype(bf16)

    def grad_input(which, wait, state, inverse, coef, grad_f):
        inv = widen(spread(inverse), PART // 128)
        rest = grad_f - state.astype(f32) * widen(spread(coef), PART // 128)
        return (rest + inv * gain * rows_product(which, query_product, wait)).astype(bf16)

    grad3 = grad_input(2, False, state3[...], inverse3, coef3, cot_ref[...].astype(f32))
    drain()
    rows_forward(3)
    inner2 = stat_sum(3)
    coef2 = inverse2 * inverse2 * inverse2 * inner2 * (1.0 / D)
    grad_ref[...] = grad_input(3, True, x_ref[...], inverse2, coef2, grad3.astype(f32))
    drain()


def shards(hidden, keys, values, norm_gain, w_query, w_out, depth, cotangent):
    any_spec = pl.BlockSpec(memory_space=pl.ANY)
    vmem_spec = pl.BlockSpec(memory_space=pltpu.VMEM)
    sem = pltpu.SemaphoreType.DMA
    out = jax.ShapeDtypeStruct((TOK, PART), bf16)
    return pl.pallas_call(
        kernel,
        out_shape=(out, out),
        in_specs=[any_spec] * 6 + [pl.BlockSpec(memory_space=pltpu.SMEM), any_spec],
        out_specs=(vmem_spec, vmem_spec),
        scratch_shapes=[
            pltpu.VMEM((TOK, PART), bf16),
            pltpu.VMEM((1, PART), f32),
            pltpu.VMEM((PART, HEADS), bf16),
            pltpu.VMEM((HEADS, PART), bf16),
            pltpu.VMEM((TOK, PART), bf16),
            pltpu.VMEM((N_Y, N_Z, TOK, HD), bf16),
            pltpu.VMEM((N_Y, N_Z, TOK, HD), bf16),
            pltpu.VMEM((N_Y, ROWS, CHUNK), f32),
            pltpu.VMEM((2, N_Y, ROWS, CHUNK), bf16),
            pltpu.VMEM((ROWS, 128), f32),
            pltpu.VMEM((3, HEADS, HD), bf16),
            pltpu.VMEM((3, N_MP, ROWS, HD), bf16),
            pltpu.VMEM((4, 8, TOK), f32),
            pltpu.VMEM((4, N_MP, 8, TOK), f32),
            pltpu.VMEM((4, N_MP, TOK, ROWS), bf16),
            pltpu.VMEM((128, PART), bf16),
            pltpu.VMEM((N_MP, 4, TILE, HD), bf16),
            pltpu.VMEM((N_MP, 4, TILE, HD), bf16),
            pltpu.VMEM((4, N_Y, N_Z, TILE, HD), bf16),
            pltpu.VMEM((TOK, PART), bf16),
            sem((7,)),
            sem((3, 4, 5)), sem((3, 4, 5)),
            sem((4, 14)), sem((4, 14)), sem((2, 4, 7)), sem((2, 4, 7)),
            sem((3, 8)), sem((3, 8)), sem((4, 8)), sem((4, 8)), sem((4, 8)), sem((4, 8)),
            sem((8,)), sem((8,)),
        ],
        compiler_params=pltpu.CompilerParams(
            collective_id=0, has_side_effects=True, vmem_limit_bytes=60 * 1024 * 1024
        ),
        name="recursion",
    )(hidden, keys, values, norm_gain.reshape(1, PART), w_query, w_out, depth, cotangent)


def solution(mesh):
    return jax.shard_map(
        shards,
        mesh=mesh,
        in_specs=(
            P("seq", "mp"),
            P("seq", "mp"),
            P("seq", "mp"),
            P("mp"),
            P("mp", None),
            P(None, "mp"),
            P("seq"),
            P("seq", "mp"),
        ),
        out_specs=(P("seq", "mp"), P("seq", "mp")),
        check_vma=False,
    )
```

time: 107 us -> 103 us (0.963)
  Pallas kernels: 103 us -> 98 us
    pallas_call x1, Pallas kernels: 103 us -> 98 us  [shards(): pl.pallas_call(kernel, out_shape=(out, out), in_specs=[any_spec] * 6 + [p...]
where the time goes in v2:
time: 103 us; the launch traced here: 102 us
  Pallas kernels  98 us (95%)
  local copies, waits for them, and re-layouts  3.14 us (3%)
  between operations  1.29 us (1%)
    pallas_call x1, Pallas kernels, shards(): pl.pallas_call(kernel, out_shape=(out, out), in_specs=[any_spec] * 6 + [p...  98 us
    unnamed x2, local copies, waits for them, and re-layouts  3.14 us

profile of v2, /device:TPU:57, one launch (start us, length us, event | category | flops | bytes accessed | tf_op | source)
XLA Modules:
  0.0 102.4 jit_solution(1297698276400274333)
XLA Ops:
  1.3 98.0 %recursion.1 = (bf16[128,512]{1,0:T(8,128)(2,1)}, bf16[128,512]{1,0:T(8,128)(2,1)}) custom-call(bf16[128,512]{1,0:T(8,128)(2,1)} %x_hbm.1, bf16[128,128]{1,0:T(8,128)(2,1)} %k_hbm.1, bf16[128,128]{1,0:T(8,128)(2,1)} %v_hbm.1, f32[1,512]{1,0:T(1,128)} %bitcast.1, bf16[512,2048]{1,0:T(8,128)(2,1)} %wq_hbm.1, bf16[2048,512]{1,0:T(8,128)(2,1)} %wo_hbm.1, ...), custom_call_target="tpu_custom_call" | custom-call | tf_op jit(solution)/shard_map/recursion/pallas_call | solution.py:529
  99.3 1.6 %copy.13 = bf16[128,512]{1,0:T(8,128)(2,1)} copy(bf16[128,512]{1,0:T(8,128)(2,1)} %get-tuple-element.4) | data formatting | bytes 262144
  100.9 1.6 %copy.14 = bf16[128,512]{1,0:T(8,128)(2,1)} copy(bf16[128,512]{1,0:T(8,128)(2,1)} %get-tuple-element.5) | data formatting | bytes 262144

commit v3 on v2

--- a/solution.py
+++ b/solution.py
@@ -86,6 +86,7 @@
     turned, tile_buf, tile_recv, tiles,
     state3,
     load_sem, first_send, first_recv,
+    tile_first_send, tile_first_recv,
     ring_send, ring_recv, tile_ring_send, tile_ring_recv,
     part_send_sem, part_recv_sem, stat_send_sem, stat_recv_sem, rows_send_sem, rows_recv_sem,
     tile_send_sem, tile_recv_sem,
@@ -113,9 +114,10 @@
 
     targets = (at(y, (z + 1) % N_Z, me), at(y, (z + 7) % N_Z, me), at((y + 1) % N_Y, z, me), at((y + 7) % N_Y, z, me))
     barrier = pltpu.get_barrier_semaphore()
-    for target in targets + tuple(at(y, z, (me + k) % N_MP) for k in range(1, 8)):
-        pl.semaphore_signal(barrier, inc=1, device_id=target, device_id_type=MESH)
-    pl.semaphore_wait(barrier, 11)
+    for k in NEAR:
+        for target in (at(y, (z + k) % N_Z, me), at((y + k) % N_Y, z, me), at(y, z, (me + k) % N_MP)):
+            pl.semaphore_signal(barrier, inc=1, device_id=target, device_id_type=MESH)
+    pl.semaphore_wait(barrier, 21)
 
     def send(src, dst, send_sem, recv_sem, target):
         copy = pltpu.make_async_remote_copy(
@@ -148,11 +150,31 @@
             ref = first_piece(gather, stream, step, 1)
             send(ref, ref, gather[2].at[stream, step], gather[3].at[stream, step], targets[stream])
 
+    def first_own(gather):
+        first_start(gather, 1)
+        two = (at(y, (z + 2) % N_Z, me), at(y, (z + 6) % N_Z, me), at((y + 2) % N_Y, z, me), at((y + 6) % N_Y, z, me))
+        for stream in range(4):
+            ref = first_piece(gather, stream, 2, 2)
+            send(ref, ref, gather[2].at[stream, 2], gather[3].at[stream, 2], two[stream])
+
+    def first_all(gather):
+        for k in NEAR:
+            for i, target in enumerate((at(y, (z + k) % N_Z, me), at((y + k) % N_Y, z, me))):
+                ref = gather[0][i].at[y, z]
+                send(ref, ref, gather[2].at[i, k], gather[3].at[i, (z, y)[i]], target)
+
+    def first_all_wait(gather):
+        for k in NEAR:
+            for i in range(2):
+                other = ((z, y)[i] + k) % 8
+                where = (y, other) if i == 0 else (other, z)
+                arrived(gather[0][i].at[where], gather[2].at[i, 0], gather[3].at[i, other], at(*where, me))
+
     def first_turn(gather, step):
         for stream in range(4):
             ref = first_piece(gather, stream, step, 0)
             arrived(ref, gather[2].at[stream, step], gather[3].at[stream, step], targets[stream ^ 1])
-        if step < 4:
+        if step in (2, 3):
             first_start(gather, step + 1)
 
     def piece(gather, stream, unit, shift):
@@ -188,9 +210,9 @@
             if (step + 1, part) in units:
                 ring_start(gather, stream, (step + 1, part))
 
-    kv = ((kbuf, vbuf), 4, first_send.at[0], first_recv.at[0], ring_send, ring_recv)
-    tile_f = ((tiles.at[0], tiles.at[1]), 2, first_send.at[1], first_recv.at[1], tile_ring_send.at[0], tile_ring_recv.at[0])
-    tile_b = ((tiles.at[2], tiles.at[3]), 2, first_send.at[2], first_recv.at[2], tile_ring_send.at[1], tile_ring_recv.at[1])
+    kv = ((kbuf, vbuf), 4, first_send, first_recv, ring_send, ring_recv)
+    tile_f = ((tiles.at[0], tiles.at[1]), 2, tile_first_send.at[0], tile_first_recv.at[0], tile_ring_send.at[0], tile_ring_recv.at[0])
+    tile_b = ((tiles.at[2], tiles.at[3]), 2, tile_first_send.at[1], tile_first_recv.at[1], tile_ring_send.at[1], tile_ring_recv.at[1])
 
     def part_send(which, peer, k):
         send(
@@ -376,7 +398,7 @@
 
     loads[0].wait()
     loads[1].wait()
-    first_start(kv, 1)
+    first_own(kv)
     for load in loads[2:5]:
         load.wait()
     x_f = x_ref[...].astype(f32)
@@ -426,50 +448,41 @@
         tile = tile + tile_recv[peer].astype(f32)
     for i in range(4):
         tiles[i, y, z] = tile[i].astype(bf16)
-    first_start(tile_f, 1)
+    first_all(tile_f)
     ring_turn(kv, 6)
     grad_att3 = part_sum(1)
     ring_turn(kv, 7)
-    first_turn(tile_f, 1)
-    first_start(tile_b, 1)
     step_scores(query2, 2)
     ring_turn(kv, 8)
-    first_turn(tile_f, 2)
     ring_turn(kv, 9)
-    first_turn(tile_b, 1)
     ring_turn(kv, 10)
-    first_turn(tile_f, 3)
+    ring_turn(kv, 11)
+    first_all_wait(tile_f)
     inject(tile_f, 0)
-    ring_turn(kv, 11)
-    first_turn(tile_f, 4)
     inject(tile_f, 1)
     step_scores(query2, 3)
     ring_turn(kv, 12)
     ring_turn(kv, 13)
     step_scores(query2, 4)
 
-    ring_turn(tile_f, 0)
-    ring_turn(tile_f, 1)
     attended2, share2 = weigh(0, None)
     rows_start(0, side(attended2))
-    ring_turn(tile_f, 2)
-    ring_turn(tile_f, 3)
-    first_turn(tile_b, 2)
-    drain()
+    for index in range(4):
+        ring_turn(tile_f, index)
+    first_all(tile_b)
     rows_forward(0)
     ring_turn(tile_f, 4)
-    first_turn(tile_b, 3)
-    inject(tile_b, 0)
+    ring_turn(tile_f, 5)
     x3 = (x_ref[...].astype(f32) + live2 * rows_product(0, out_product)).astype(bf16)
     state3[...] = x3
     x3_f = x3.astype(f32)
     stat_start(1, row_stat(x3_f * x3_f))
 
     project(2, grad_cols(x3))
-    first_turn(tile_b, 4)
+    ring_turn(tile_f, 6)
+    first_all_wait(tile_b)
+    inject(tile_b, 0)
     inject(tile_b, 1)
-    ring_turn(tile_f, 5)
-    ring_turn(tile_f, 6)
     raw3 = raw2 + live2 * rows_product(0, tile_product(0), wait=False)
     query3 = (raw3 * (SCALE * LOG2E)).astype(bf16)
     own_scores(query3)
@@ -553,7 +566,7 @@
             pltpu.VMEM((4, N_Y, N_Z, TILE, HD), bf16),
             pltpu.VMEM((TOK, PART), bf16),
             sem((7,)),
-            sem((3, 4, 5)), sem((3, 4, 5)),
+            sem((4, 5)), sem((4, 5)), sem((2, 2, 8)), sem((2, 2, 8)),
             sem((4, 14)), sem((4, 14)), sem((2, 4, 7)), sem((2, 4, 7)),
             sem((3, 8)), sem((3, 8)), sem((4, 8)), sem((4, 8)), sem((4, 8)), sem((4, 8)),
             sem((8,)), sem((8,)),

time: 103 us -> 96.5 us (0.937)
  Pallas kernels: 98 us -> 91.9 us
    pallas_call x1, Pallas kernels: 98 us -> 91.9 us  [shards(): pl.pallas_call(kernel, out_shape=(out, out), in_specs=[any_spec] * 6 + [p...]
where the time goes in v3:
time: 96.5 us; the launch traced here: 96.3 us
  Pallas kernels  91.9 us (95%)
  local copies, waits for them, and re-layouts  3.14 us (3%)
  between operations  1.29 us (1%)
    pallas_call x1, Pallas kernels, shards(): pl.pallas_call(kernel, out_shape=(out, out), in_specs=[any_spec] * 6 + [p...  91.9 us
    unnamed x2, local copies, waits for them, and re-layouts  3.14 us

profile of v3, /device:TPU:57, one launch (start us, length us, event | category | flops | bytes accessed | tf_op | source)
XLA Modules:
  0.0 96.3 jit_solution(17059406329639785323)
XLA Ops:
  1.3 91.9 %recursion.1 = (bf16[128,512]{1,0:T(8,128)(2,1)}, bf16[128,512]{1,0:T(8,128)(2,1)}) custom-call(bf16[128,512]{1,0:T(8,128)(2,1)} %x_hbm.1, bf16[128,128]{1,0:T(8,128)(2,1)} %k_hbm.1, bf16[128,128]{1,0:T(8,128)(2,1)} %v_hbm.1, f32[1,512]{1,0:T(1,128)} %bitcast.1, bf16[512,2048]{1,0:T(8,128)(2,1)} %wq_hbm.1, bf16[2048,512]{1,0:T(8,128)(2,1)} %wo_hbm.1, ...), custom_call_target="tpu_custom_call" | custom-call | tf_op jit(solution)/shard_map/recursion/pallas_call | solution.py:542
  93.2 1.6 %copy.13 = bf16[128,512]{1,0:T(8,128)(2,1)} copy(bf16[128,512]{1,0:T(8,128)(2,1)} %get-tuple-element.4) | data formatting | bytes 262144
  94.8 1.6 %copy.14 = bf16[128,512]{1,0:T(8,128)(2,1)} copy(bf16[128,512]{1,0:T(8,128)(2,1)} %get-tuple-element.5) | data formatting | bytes 262144

commit v4 on v3

--- a/solution.py
+++ b/solution.py
@@ -152,10 +152,9 @@
 
     def first_own(gather):
         first_start(gather, 1)
-        two = (at(y, (z + 2) % N_Z, me), at(y, (z + 6) % N_Z, me), at((y + 2) % N_Y, z, me), at((y + 6) % N_Y, z, me))
         for stream in range(4):
             ref = first_piece(gather, stream, 2, 2)
-            send(ref, ref, gather[2].at[stream, 2], gather[3].at[stream, 2], two[stream])
+            send(ref, ref, gather[2].at[stream, 2], gather[3].at[stream, 2], two_away[stream])
 
     def first_all(gather):
         for k in NEAR:
@@ -182,11 +181,8 @@
         away = (1 if stream % 2 == 0 else -1) * (unit[0] - shift)
         width = 8 // parts
         mine, across = (z, y) if stream < 2 else (y, z)
-        if parts == 4:
-            toward = 2 * (mine % 2) - 1
-            turn = (0, toward, -toward, 2)[unit[1]]
-        else:
-            turn = unit[1]
+        toward = 2 * (mine % 2) - 1
+        turn = (0, toward, -toward, 2)[unit[1]]
         span = pl.ds((mine // width + parts + turn) % parts * width, width)
         if stream < 2:
             return bufs[0].at[(across + 8 - away) % N_Y, span]
@@ -210,9 +206,43 @@
             if (step + 1, part) in units:
                 ring_start(gather, stream, (step + 1, part))
 
+    two_away = (at(y, (z + 2) % N_Z, me), at(y, (z + 6) % N_Z, me), at((y + 2) % N_Y, z, me), at((y + 6) % N_Y, z, me))
+
+    def chunk(gather, stream, step, shift):
+        away = (1 if stream % 2 == 0 else -1) * (step - shift)
+        span = pl.ds(stream % 2 * 4, 4) if step == 4 else pl.ds(0, 8)
+        if stream < 2:
+            return gather[0][0].at[(y + 8 - away) % N_Y, span]
+        return gather[0][1].at[span, (z + 8 - away) % N_Z]
+
+    def chunk_send(gather, stream, step, shift):
+        ref = chunk(gather, stream, step, shift)
+        target = (two_away if shift == 2 else targets)[stream ^ 2]
+        send(ref, ref, gather[4].at[stream, step], gather[5].at[stream, step], target)
+
+    def chunk_wait(gather, step):
+        for stream in range(4):
+            ref = chunk(gather, stream, step, 0)
+            arrived(ref, gather[4].at[stream, step], gather[5].at[stream, step], targets[stream ^ 3])
+
+    def second_start(gather):
+        for step in (1, 2):
+            for stream in range(4):
+                chunk_send(gather, stream, step, step)
+
+    def second_turn(gather):
+        chunk_wait(gather, 2)
+        for step in (3, 4):
+            for stream in range(4):
+                chunk_send(gather, stream, step, step - 2)
+
+    def second_wait(gather):
+        for step in (1, 3, 4):
+            chunk_wait(gather, step)
+
     kv = ((kbuf, vbuf), 4, first_send, first_recv, ring_send, ring_recv)
-    tile_f = ((tiles.at[0], tiles.at[1]), 2, tile_first_send.at[0], tile_first_recv.at[0], tile_ring_send.at[0], tile_ring_recv.at[0])
-    tile_b = ((tiles.at[2], tiles.at[3]), 2, tile_first_send.at[1], tile_first_recv.at[1], tile_ring_send.at[1], tile_ring_recv.at[1])
+    tile_f = ((tiles.at[0], tiles.at[1]), 1, tile_first_send.at[0], tile_first_recv.at[0], tile_ring_send.at[0], tile_ring_recv.at[0])
+    tile_b = ((tiles.at[2], tiles.at[3]), 1, tile_first_send.at[1], tile_first_recv.at[1], tile_ring_send.at[1], tile_ring_recv.at[1])
 
     def part_send(which, peer, k):
         send(
@@ -282,10 +312,10 @@
             total = total + product(rows_recv[which, source], source)
         return total
 
-    def drain():
-        for copy in pending:
+    def drain(until=None):
+        for copy in pending[:until]:
             copy.wait_send()
-        pending.clear()
+        del pending[:until]
 
     def project(which, product, peers=ORDER + (0,)):
         for k in peers:
@@ -366,12 +396,16 @@
     def backward(level, grad_att, attended, share):
         delta = jnp.sum(grad_att.astype(f32) * attended.astype(f32), axis=1, keepdims=True)
 
-        def turn(c, accum):
+        def grads(c):
             dprobs = dot_t(grad_att, values_at(c))
             ds = (pbuf[level, c].astype(f32) * (dprobs - delta)).astype(bf16)
-            return accum + dot(ds, keys_at(c))
-
-        accum = lax.fori_loop(0, y + 1, turn, jnp.zeros((ROWS, HD), f32))
+            return dot(ds, keys_at(c))
+
+        count = y + 1
+        accum = lax.fori_loop(
+            0, count // 2, lambda i, a: a + grads(2 * i) + grads(2 * i + 1), jnp.zeros((ROWS, HD), f32)
+        )
+        accum = lax.fori_loop(count // 2 * 2, count, lambda c, a: a + grads(c), accum)
         return (accum * (share * SCALE)).astype(bf16)
 
     def head_cols(j):
@@ -453,61 +487,66 @@
     grad_att3 = part_sum(1)
     ring_turn(kv, 7)
     step_scores(query2, 2)
+    mark = len(pending)
     ring_turn(kv, 8)
+    drain(mark // 2)
     ring_turn(kv, 9)
     ring_turn(kv, 10)
     ring_turn(kv, 11)
     first_all_wait(tile_f)
-    inject(tile_f, 0)
-    inject(tile_f, 1)
+    mark = len(pending)
+    second_start(tile_f)
     step_scores(query2, 3)
     ring_turn(kv, 12)
+    drain(mark - 16)
     ring_turn(kv, 13)
     step_scores(query2, 4)
 
     attended2, share2 = weigh(0, None)
     rows_start(0, side(attended2))
-    for index in range(4):
-        ring_turn(tile_f, index)
-    first_all(tile_b)
+    second_turn(tile_f)
     rows_forward(0)
-    ring_turn(tile_f, 4)
-    ring_turn(tile_f, 5)
     x3 = (x_ref[...].astype(f32) + live2 * rows_product(0, out_product)).astype(bf16)
     state3[...] = x3
     x3_f = x3.astype(f32)
     stat_start(1, row_stat(x3_f * x3_f))
 
+    first_all(tile_b)
     project(2, grad_cols(x3))
-    ring_turn(tile_f, 6)
-    first_all_wait(tile_b)
-    inject(tile_b, 0)
-    inject(tile_b, 1)
+    second_wait(tile_f)
     raw3 = raw2 + live2 * rows_product(0, tile_product(0), wait=False)
     query3 = (raw3 * (SCALE * LOG2E)).astype(bf16)
     own_scores(query3)
 
-    def score_turn(c, carry):
+    first_all_wait(tile_b)
+    second_start(tile_b)
+
+    def score_two(i, carry):
+        first, second = dot_t(query3, keys_at(2 * i)), dot_t(query3, keys_at(2 * i + 1))
+        sbuf[2 * i] = first
+        sbuf[2 * i + 1] = second
+        best_ref[...] = jnp.maximum(best_ref[...], jnp.maximum(lane_max(first), lane_max(second)))
+        return carry
+
+    def score_one(c, carry):
         scores(query3, c)
         return carry
 
-    lax.fori_loop(0, y, score_turn, 0)
-    ring_turn(tile_b, 0)
-    ring_turn(tile_b, 1)
+    lax.fori_loop(0, y // 2, score_two, 0)
+    lax.fori_loop(y // 2 * 2, y, score_one, 0)
+    mark = len(pending)
     inverse3 = inverse_of(1)
     factor3 = twice(spread(inverse3))[:, :1]
     attended3, share3 = weigh(1, factor3)
-    ring_turn(tile_b, 2)
-    ring_turn(tile_b, 3)
     grad_query3 = backward(1, (grad_att3 * live3).astype(bf16), attended3, share3)
     rows_start(2, side(grad_query3))
     stat_start(2, row_stat(side(grad_query3.astype(f32) * raw3)))
-    ring_turn(tile_b, 4)
-    ring_turn(tile_b, 5)
-    drain()
+    second_turn(tile_b)
+    state_part = part_sum(2)
+    drain(mark // 2)
     rows_forward(2)
-    ring_turn(tile_b, 6)
-    state_part = part_sum(2)
+    drain(mark - mark // 2)
+    second_wait(tile_b)
 
     through = rows_product(2, tile_product(2))
     inner3 = stat_sum(2)
@@ -515,6 +554,7 @@
     grad_att2 = live2 * (grad_att3 + twice(spread(inverse3)) * through - twice(spread(coef3)) * state_part)
     rows_start(1, side(attended3))
     grad_query2 = backward(0, grad_att2.astype(bf16), attended2, share2)
+    mark = len(pending)
     rows_start(3, side(grad_query2))
     stat_start(3, row_stat(side(grad_query2.astype(f32) * raw2)))
     rows_forward(1)
@@ -526,7 +566,7 @@
         return (rest + inv * gain * rows_product(which, query_product, wait)).astype(bf16)
 
     grad3 = grad_input(2, False, state3[...], inverse3, coef3, cot_ref[...].astype(f32))
-    drain()
+    drain(mark)
     rows_forward(3)
     inner2 = stat_sum(3)
     coef2 = inverse2 * inverse2 * inverse2 * inner2 * (1.0 / D)
@@ -539,7 +579,7 @@
     vmem_spec = pl.BlockSpec(memory_space=pltpu.VMEM)
     sem = pltpu.SemaphoreType.DMA
     out = jax.ShapeDtypeStruct((TOK, PART), bf16)
-    return pl.pallas_call(
+    mixed, grad = pl.pallas_call(
         kernel,
         out_shape=(out, out),
         in_specs=[any_spec] * 6 + [pl.BlockSpec(memory_space=pltpu.SMEM), any_spec],
@@ -567,7 +607,7 @@
             pltpu.VMEM((TOK, PART), bf16),
             sem((7,)),
             sem((4, 5)), sem((4, 5)), sem((2, 2, 8)), sem((2, 2, 8)),
-            sem((4, 14)), sem((4, 14)), sem((2, 4, 7)), sem((2, 4, 7)),
+            sem((4, 14)), sem((4, 14)), sem((2, 4, 5)), sem((2, 4, 5)),
             sem((3, 8)), sem((3, 8)), sem((4, 8)), sem((4, 8)), sem((4, 8)), sem((4, 8)),
             sem((8,)), sem((8,)),
         ],
@@ -576,6 +616,8 @@
         ),
         name="recursion",
     )(hidden, keys, values, norm_gain.reshape(1, PART), w_query, w_out, depth, cotangent)
+    live = depth[0] >= 2
+    return jnp.where(live, mixed, hidden), jnp.where(live, grad, cotangent)
 
 
 def solution(mesh):

time: 96.5 us -> 90.7 us (0.940)
  Pallas kernels: 91.9 us -> 86.9 us
  local copies, waits for them, and re-layouts: 3.14 us -> 0.01 us
  other arithmetic: 0 us -> 1.7 us
    pallas_call x1, Pallas kernels: 91.9 us -> 86.9 us  [shards(): pl.pallas_call(kernel, out_shape=(out, out), in_specs=[any_spec] * 6 + [p...]
    unnamed x2 -> x4, local copies, waits for them, and re-layouts: 3.14 us -> 0.01 us
    select_n x0 -> x1, other arithmetic: none -> 1.7 us  [shards(): return (jnp.where(live, mixed, hidden), jnp.where(live, grad, cotangent))]
where the time goes in v4:
time: 90.7 us; the launch traced here: 89.9 us
  Pallas kernels  86.9 us (96%)
  other arithmetic  1.7 us (2%)
  between operations  1.32 us (1%)
    pallas_call x1, Pallas kernels, shards(): pl.pallas_call(kernel, out_shape=(out, out), in_specs=[any_spec] * 6 + [p...  86.9 us

profile of v4, /device:TPU:57, one launch (start us, length us, event | category | flops | bytes accessed | tf_op | source)
XLA Modules:
  0.0 89.9 jit_solution(1542187988170536775)
XLA Ops:
  1.3 0.0 copy-start
  1.3 0.0 copy-start.1
  1.3 86.9 %recursion.1 = (bf16[128,512]{1,0:T(8,128)(2,1)}, bf16[128,512]{1,0:T(8,128)(2,1)}) custom-call(bf16[128,512]{1,0:T(8,128)(2,1)} %x_hbm.1, bf16[128,128]{1,0:T(8,128)(2,1)} %k_hbm.1, bf16[128,128]{1,0:T(8,128)(2,1)} %v_hbm.1, f32[1,512]{1,0:T(1,128)} %bitcast.2, bf16[512,2048]{1,0:T(8,128)(2,1)} %wq_hbm.1, bf16[2048,512]{1,0:T(8,128)(2,1)} %wo_hbm.1, ...), custom_call_target="tpu_custom_call" | custom-call | tf_op jit(solution)/shard_map/recursion/pallas_call | solution.py:582
  88.2 0.0 copy-done
  88.2 0.0 copy-done.1
  88.2 1.7 %broadcast_select_fusion = (bf16[128,512]{1,0:T(8,128)(2,1)}, bf16[128,512]{1,0:T(8,128)(2,1)}) fusion(bf16[128,512]{1,0:T(8,128)(2,1)} %get-tuple-element.5, bf16[128,512]{1,0:T(8,128)(2,1)S(1)} %copy-done.1, pred[]{:T(512)} %bitcast, bf16[128,512]{1,0:T(8,128)(2,1)} %get-tuple-element.4, bf16[128,512]{1,0:T(8,128)(2,1)S(1)} %copy-done), kind=kLoop, calls=%fused_computation | loop fusion | flops 131072 | bytes 786433 | tf_op jit(solution)/shard_map/jit(_where)/select_n | solution.py:620
Async XLA Ops:
  1.3 86.9 %copy-start = (bf16[128,512]{1,0:T(8,128)(2,1)S(1)}, bf16[128,512]{1,0:T(8,128)(2,1)}, u32[]{:S(2)}) copy-start(bf16[128,512]{1,0:T(8,128)(2,1)} %x_hbm.1) | copy-start | bytes 393220
  1.3 86.9 %copy-start.1 = (bf16[128,512]{1,0:T(8,128)(2,1)S(1)}, bf16[128,512]{1,0:T(8,128)(2,1)}, u32[]{:S(2)}) copy-start(bf16[128,512]{1,0:T(8,128)(2,1)} %cot_hbm.1) | copy-start | bytes 393220
